TPU v7x, 512 devices: a whole 4x8x8 slice. The times are simulated.
512 devices in a mesh: slab: 4 (over y_lo, core), energy: 128 (over y_hi, z, x).
Axes of the slice: x: 4, y: 8 (y_hi: 4, y_lo: 2; y = y_hi * 2 + y_lo), z: 8, core: 2. Of those that a mesh axis runs over, the one named last changes fastest.
Arguments:
- mode_energy: float32 [2048], replicated, may hold values from -2.5 to 2.5
- levels: int32 [8], P('slab'), may hold values from 0 to 7
- energy_jitter: int32 [256], P('energy'), may hold values from 0 to 7
- offsets: int32 [128], replicated, may hold values from 0 to 255
- scattering: float32 [2, 256, 8, 2048], P(None, 'energy', 'slab'), may hold values from -1.5 to 1.5, as said below
Outputs:
- density: float32 [256, 8, 2048], P('energy', 'slab')
- polarization: float32 [128, 8, 2048], P('energy', 'slab')
Inputs may be any that keep to these rules, and one draw needn't show every extreme that they name: scattering[1] (the imaginary part) lies between -0.3 and -0.01; scattering[0] between -1.5 and 1.5.
All inputs are finite; a program needn't handle non-finite values.
Results may differ from a plain program's by a relative error of at most 0.0003.
Values sent between devices are 32-bit elements; how exact they have to be, the bound alone decides.
A program may use at most 64 MiB of HBM per device.

v0:
```python
import math

import jax
import jax.numpy as jnp
from jax import lax
from jax.sharding import Mesh
from jax.sharding import PartitionSpec as P

FINE = 8
SLAB = ("slab_0", "slab_1")


ETA = 0.1
GAMMA = 0.5
KT = 0.25
STEP_V = 0.15
E_LOW = -3.0
E_SPAN = 6.0


def cut_along(array, dim, devices):
    shape = array.shape
    blocks = array.reshape(*shape[:dim], devices, shape[dim] // devices, *shape[dim + 1 :])
    return jnp.moveaxis(blocks, dim, 0)


def laid_out(blocks, dim):
    shape = list(blocks.shape[1:])
    shape[dim] *= blocks.shape[0]
    return jnp.moveaxis(blocks, 0, dim).reshape(shape)


def moved_by_axis(blocks, axes, sequence):
    inside = blocks.shape[1:]
    result = blocks.reshape(*(lax.axis_size(a) for a in axes), *inside)
    for k in sequence:
        result = lax.all_to_all(result, axes[k], k, k, tiled=True)
    return result.reshape(-1, *inside)


def exchange_by_chip(array, groups, sequence, split_dim, concat_dim):
    devices = lax.axis_size(groups[0]) * lax.axis_size(groups[1])
    blocks = cut_along(array, split_dim, devices)
    return laid_out(moved_by_axis(blocks, groups, sequence), concat_dim)


def invert(real_part, imag_part):
    denom = real_part * real_part + imag_part * imag_part
    return (real_part / denom, -imag_part / denom)


def sweep_layers(start_re, start_im, a_re, a_im, order):
    incoming = {}
    g_re, g_im = (start_re, start_im)
    for layer in order:
        incoming[layer] = (g_re, g_im)
        g_re, g_im = invert(a_re[:, layer] - g_re, a_im[:, layer] - g_im)
    return (incoming, g_re, g_im)


def edge_spectral(left_re, left_im, right_re, right_im, a_re, a_im):
    layer_total = a_re.shape[1]
    forward = list(range(layer_total))
    backward = list(reversed(range(layer_total)))
    left_in, unused_a, unused_b = sweep_layers(left_re, left_im, a_re, a_im, forward)
    right_in, unused_c, unused_d = sweep_layers(right_re, right_im, a_re, a_im, backward)
    side_re = jnp.stack([left_in[layer][0] + right_in[layer][0] for layer in forward], axis=1)
    side_im = jnp.stack([left_in[layer][1] + right_in[layer][1] for layer in forward], axis=1)
    green_re, green_im = invert(a_re - side_re, a_im - side_im)
    return -2.0 * green_im


def local(mode_energy, levels, energy_jitter, offsets, scattering):
    e_dev = energy_jitter.shape[0]
    n_energy = lax.axis_size("energy")
    points = e_dev * n_energy
    grid_pos = lax.axis_index("energy") * e_dev + jnp.arange(e_dev, dtype=jnp.int32)
    energy = E_LOW + E_SPAN * (FINE * grid_pos + energy_jitter).astype(jnp.float32) / (
        FINE * points
    )
    potential = STEP_V * levels.astype(jnp.float32)
    a_re = (
        energy[:, None, None]
        - mode_energy[None, None, :]
        - potential[None, :, None]
        - scattering[0]
    )
    a_im = ETA - scattering[1]
    coeffs = jnp.stack((a_re, a_im))
    moved = exchange_by_chip(coeffs, ("slab_0", "slab_1"), (1, 0), 3, 2)
    block_plane = (e_dev, moved.shape[3])
    start_re = jnp.zeros(block_plane, jnp.float32)
    start_im = jnp.full(block_plane, -GAMMA, jnp.float32)
    block_spectral = edge_spectral(start_re, start_im, start_re, start_im, moved[0], moved[1])
    spectral = lax.all_to_all(block_spectral, SLAB, split_axis=1, concat_axis=2, tiled=True)
    occupation = 1.0 / (1.0 + jnp.exp(energy / KT))
    density = occupation[:, None, None] * spectral
    hole_part = (1.0 - occupation[:, None, None]) * spectral
    offset_count = offsets.shape[0]
    freq = jnp.arange(points, dtype=jnp.int32)
    phase_idx = freq[:, None] * freq[None, :] % points
    angle = 2.0 * math.pi / points * phase_idx.astype(jnp.float32)
    cos_table = jnp.cos(angle)
    sin_table = jnp.sin(angle)
    offset_phase = offsets[:, None] * freq[None, :] % points
    offset_angle = 2.0 * math.pi / points * offset_phase.astype(jnp.float32)
    cos_offset = jnp.cos(offset_angle)
    sin_offset = jnp.sin(offset_angle)
    stacked = jnp.stack((density, hole_part), axis=1)
    spectra = lax.all_to_all(stacked, "energy", split_axis=3, concat_axis=0, tiled=True)
    item_count = spectra.shape[2]
    width = spectra.shape[3]
    flattened = spectra.reshape(points, 2 * item_count * width)
    real_tr = jnp.dot(cos_table, flattened, precision=lax.Precision.HIGHEST).reshape(
        points, 2, item_count * width
    )
    imag_tr = -jnp.dot(sin_table, flattened, precision=lax.Precision.HIGHEST).reshape(
        points, 2, item_count * width
    )
    cross_re = real_tr[:, 0] * real_tr[:, 1] + imag_tr[:, 0] * imag_tr[:, 1]
    cross_im = imag_tr[:, 0] * real_tr[:, 1] - real_tr[:, 0] * imag_tr[:, 1]
    summed = jnp.dot(cos_offset, cross_re, precision=lax.Precision.HIGHEST) - jnp.dot(
        sin_offset, cross_im, precision=lax.Precision.HIGHEST
    )
    offset_table = (summed / (points * points)).reshape(offset_count, item_count, width)
    polarization = lax.all_to_all(offset_table, "energy", split_axis=0, concat_axis=2, tiled=True)
    return (density, polarization)


def solution(mesh):
    split = Mesh(mesh.devices.reshape(2, 2, mesh.shape["energy"]), ("slab_0", "slab_1", "energy"))
    placed = (P(), P(SLAB), P("energy"), P(), P(None, "energy", SLAB, None))
    return jax.shard_map(
        local,
        mesh=split,
        in_specs=placed,
        out_specs=(P("energy", SLAB, None), P("energy", SLAB, None)),
        check_vma=False,
    )
```

profile of v0, /device:TPU:1, one launch (start us, length us, event | category | flops | bytes accessed | tf_op | source)
XLA Modules:
  0.0 107.0 jit_solution(9603509063344532424)
XLA Ops:
  0.6 0.7 convert_multiply_fusion
  1.3 0.7 broadcast_subtract_fusion.1
  2.0 0.8 broadcast_subtract_fusion
  2.7 0.9 slice_subtract_fusion.1
  3.7 10.3 %all_to_all.64 = f32[2,2,2,2,2,512]{5,3,4,0,2,1:T(2,128)S(1)} all-to-all(f32[2,2,2,2,2,512]{5,3,4,0,2,1:T(2,128)S(1)} %copy.30), channel_id=1, replica_groups=mesh['slab_0'=2,'slab_1'=2,'energy'=128] {'slab_1'}, dimensions={1} | all-to-all | bytes 131072 | tf_op jit(solution)/shard_map/all_to_all | solution.py:37
  14.0 5.3 %all_to_all.65 = f32[2,2,2,2,2,512]{5,3,4,1,2,0:T(2,128)S(1)} all-to-all(f32[2,2,2,2,2,512]{5,3,4,1,2,0:T(2,128)S(1)} %copy.31), channel_id=1, replica_groups=mesh['slab_0'=2,'slab_1'=2,'energy'=128] {'slab_0'}, dimensions={0} | all-to-all | bytes 131072 | tf_op jit(solution)/shard_map/all_to_all | solution.py:37
  19.5 0.1 constant_dynamic-update-slice_fusion.7
  19.8 0.1 fusion.33
  19.9 7.0 %all_to_all.66 = f32[2,8,512]{2,0,1:T(2,128)S(1)} all-to-all(f32[2,8,512]{2,0,1:T(2,128)S(1)} %fusion.33), channel_id=1, replica_groups=mesh['slab_0'=2,'slab_1'=2,'energy'=128] {'slab_0','slab_1'}, dimensions={1} | all-to-all | bytes 65536 | tf_op jit(solution)/shard_map/all_to_all | solution.py:95
  27.0 0.1 broadcast_multiply_fusion.1
  27.1 4.4 %copy.37 = f32[2,2,2,2048]{2,0,1,3:T(2,128)} copy(f32[2,2,2,2048]{3,2,0,1:T(2,128)S(1)} %pad_maximum_fusion.1) | data formatting | bytes 131072 | tf_op jit(solution)/shard_map/stack | solution.py:109
  31.5 6.8 %reshape.97 = f32[128,1,128]{2,1,0:T(1,128)} reshape(f32[2048,2,2,2]{3,2,1,0:T(2,128)} %bitcast.45) | data formatting | bytes 131072
  38.3 14.8 %all-to-all-start.3 = ((f32[128,1,128]{2,1,0:T(1,128)}), f32[128,1,128]{2,1,0:T(1,128)S(1)}, u32[]{:S(2)}, u32[]{:S(2)}) async-start(f32[128,1,128]{2,1,0:T(1,128)} %reshape.97), calls=%async_computation.3 | async-start | bytes 131072 | tf_op jit(solution)/shard_map/all_to_all | solution.py:110
  53.2 12.3 %all-to-all-done.3 = f32[128,1,128]{2,1,0:T(1,128)S(1)} async-done(((f32[128,1,128]{2,1,0:T(1,128)}), f32[128,1,128]{2,1,0:T(1,128)S(1)}, u32[]{:S(2)}, u32[]{:S(2)}) %all-to-all-start.3) | async-done | bytes 65568 | tf_op jit(solution)/shard_map/all_to_all | solution.py:110
  65.5 0.5 broadcast.168
  66.0 0.8 reduce
  66.8 7.8 %reshape.98 = f32[2048,2,2,2]{3,2,1,0:T(2,128)} reshape(f32[128,128]{1,0:T(8,128)S(1)} %reduce) | data formatting | bytes 131072
  74.6 0.0 copy-start
  74.6 6.7 %copy.43 = f32[2,2,2,128,16]{4,3,2,1,0:T(8,128)S(1)} copy(f32[2,2,2,128,16]{2,0,1,4,3:T(2,128)} %bitcast.46) | data formatting | bytes 131072 | tf_op jit(solution)/shard_map/all_to_all | solution.py:110
  81.3 0.4 copy.39
  81.7 0.4 reshape.93
  82.2 0.1 copy.40
  82.2 1.3 %convolution_negate_fusion = f32[256,2,32]{0,2,1:T(8,128)S(1)} fusion(f32[2,32,256]{2,1,0:T(8,128)S(1)} %bitcast.73), kind=kOutput, calls=%fused_computation | convolution fusion | flops 51265536 | bytes 131072 | tf_op jit(solution)/shard_map/dot_general | solution.py:117
  83.6 1.3 %fusion.5 = f32[256,2,32]{0,2,1:T(8,128)S(1)} fusion(f32[2,32,256]{2,1,0:T(8,128)S(1)} %bitcast.74), kind=kOutput, calls=%fused_computation.10 | convolution fusion | flops 51249152 | bytes 131072 | tf_op jit(solution)/shard_map/dot_general | solution.py:114
  84.9 0.0 copy-done
  84.9 0.8 fusion.18
  85.7 0.8 fusion
  86.5 0.8 copy.41
  87.3 6.2 %all-to-all-start.4 = ((f32[128,2,16]{2,1,0:T(2,128)}), f32[128,2,16]{2,1,0:T(2,128)S(1)}, u32[]{:S(2)}, u32[]{:S(2)}) async-start(f32[128,2,16]{2,1,0:T(2,128)} %copy.41), calls=%async_computation.4 | async-start | bytes 262144 | tf_op jit(solution)/shard_map/all_to_all | solution.py:126
  93.5 0.7 broadcast_multiply_fusion.2
  94.2 12.1 %all-to-all-done.4 = f32[128,2,16]{2,1,0:T(2,128)S(1)} async-done(((f32[128,2,16]{2,1,0:T(2,128)}), f32[128,2,16]{2,1,0:T(2,128)S(1)}, u32[]{:S(2)}, u32[]{:S(2)}) %all-to-all-start.4) | async-done | bytes 16416 | tf_op jit(solution)/shard_map/all_to_all | solution.py:126
  106.2 0.7 all_to_all.58
  (22 shorter events, 0.6 us)
Async XLA Ops:
  38.3 27.2 %all-to-all-start.3 = ((f32[128,1,128]{2,1,0:T(1,128)}), f32[128,1,128]{2,1,0:T(1,128)S(1)}, u32[]{:S(2)}, u32[]{:S(2)}) async-start(f32[128,1,128]{2,1,0:T(1,128)} %reshape.97), calls=%async_computation.3 | async-start | bytes 131072 | tf_op jit(solution)/shard_map/all_to_all | solution.py:110
  74.6 10.3 %copy-start = (s32[128]{0:T(128)S(1)}, s32[128]{0:T(128)}, u32[]{:S(2)}) copy-start(s32[128]{0:T(128)} %param.8) | copy-start | bytes 1540
  87.3 18.9 %all-to-all-start.4 = ((f32[128,2,16]{2,1,0:T(2,128)}), f32[128,2,16]{2,1,0:T(2,128)S(1)}, u32[]{:S(2)}, u32[]{:S(2)}) async-start(f32[128,2,16]{2,1,0:T(2,128)} %copy.41), calls=%async_computation.4 | async-start | bytes 262144 | tf_op jit(solution)/shard_map/all_to_all | solution.py:126
where the time goes:
time: 108 us; the launch traced here: 107 us
  local copies, waits for them, and re-layouts  28.8 us (27%)
  waiting for transfers between devices  24.4 us (23%)
  blocking collectives  22.7 us (21%)
  starting transfers between devices  20.9 us (19%)
  other arithmetic  5.01 us (5%)
  matrix products  4.27 us (4%)
    all_to_all x2, blocking collectives, moved_by_axis(): result = lax.all_to_all(result, axes[k], k, k, tiled=True)  15.7 us
    all_to_all x1, starting transfers between devices, local(): lax.all_to_all(stacked, 'energy', split_axis=3, concat_axis=0, tiled=True)  14.8 us
    unnamed x4, local copies, waits for them, and re-layouts  14.6 us
    all_to_all x1, waiting for transfers between devices, local(): lax.all_to_all(stacked, 'energy', split_axis=3, concat_axis=0, tiled=True)  12.3 us
    all_to_all x1, waiting for transfers between devices, local(): lax.all_to_all(offset_table, 'energy', split_axis=0, concat_axis=2, tiled...  12.1 us
    all_to_all x3, local copies, waits for them, and re-layouts, local(): lax.all_to_all(stacked, 'energy', split_axis=3, concat_axis=0, tiled=True)  7.61 us
    all_to_all x1, blocking collectives, local(): lax.all_to_all(block_spectral, SLAB, split_axis=1, concat_axis=2, tiled=T...  7.02 us
    all_to_all x1, starting transfers between devices, local(): lax.all_to_all(offset_table, 'energy', split_axis=0, concat_axis=2, tiled...  6.15 us
  transfers between devices with their start and end apart: 2, of which 2 were waited for; matrix products, arithmetic and copies ran while one was open for 1% of the time, Pallas kernels for 0%

commit v1 on v0

v1 whole, which is shorter than its diff:
```python
import jax
import jax.numpy as jnp
from jax import lax
from jax.experimental import pallas as pl
from jax.experimental.pallas import tpu as pltpu
from jax.sharding import PartitionSpec as P

FINE = 8
ETA = 0.1
GAMMA = 0.5
KT = 0.25
STEP_V = 0.15
E_LOW = -3.0
E_SPAN = 6.0

SLABS = 4
ENERGY = 128
POINTS = 256
LAYERS = 8
ROW = 4
BLOCKS = ENERGY // ROW
ZS = 8
LOGICAL = pl.DeviceIdType.LOGICAL


def invert(re, im):
    scale = 1.0 / (re * re + im * im)
    return re * scale, -im * scale


def interleave(first, second, odd):
    return (
        jnp.where(odd, pltpu.roll(second, 1, 0), first),
        jnp.where(odd, second, pltpu.roll(first, 7, 0)),
    )


def kernel(
    mode_hbm, levels_hbm, jitter_hbm, offsets_hbm, scat_hbm,
    dens_ref, pol_ref,
    mode, levels, jitter, offsets, scat,
    a_out, a_in, spec, spec_in, en_out, en_in, dens_out, d_all, h_all, pol_out, pol_in,
    load_sem, small_sem, slab_send, slab_recv, en_send, en_recv, spec_send, spec_recv,
    dens_send, dens_recv, pol_send, pol_recv,
):
    s = lax.axis_index("slab")
    e = lax.axis_index("energy")
    r = e // ROW
    x = lax.rem(e, ROW)
    yhi = r // ZS
    z = lax.rem(r, ZS)
    me = s * ENERGY + e

    barrier = pltpu.get_barrier_semaphore()

    def greet(i, carry):
        peer = lax.rem(e + i, ENERGY)
        pl.semaphore_signal(barrier, 1, device_id=s * ENERGY + peer, device_id_type=LOGICAL)
        return carry

    lax.fori_loop(1, ENERGY, greet, 0)
    for i in range(1, SLABS):
        peer = lax.rem(s + i, SLABS)
        pl.semaphore_signal(barrier, 1, device_id=peer * ENERGY + e, device_id_type=LOGICAL)

    def greet_sender(i, carry):
        sender = (i // ZS) * ENERGY + (s * ZS + lax.rem(i, ZS)) * ROW + x

        @pl.when(sender != me)
        def _():
            pl.semaphore_signal(barrier, 1, device_id=sender, device_id_type=LOGICAL)

        return carry

    lax.fori_loop(0, SLABS * ZS, greet_sender, 0)

    loads = [
        pltpu.make_async_copy(scat_hbm, scat, load_sem.at[0]),
        pltpu.make_async_copy(mode_hbm, mode, load_sem.at[1]),
        pltpu.make_async_copy(levels_hbm, levels, small_sem.at[0]),
        pltpu.make_async_copy(jitter_hbm, jitter, small_sem.at[1]),
        pltpu.make_async_copy(offsets_hbm, offsets, small_sem.at[2]),
    ]
    for copy in loads:
        copy.start()
    for copy in loads:
        copy.wait()

    odd = lax.rem(lax.broadcasted_iota(jnp.int32, (8, 128), 0), 2) == 1
    energy = []
    for i in range(2):
        fine = jnp.full((8, 128), FINE * (2 * e + i) + jitter[i], jnp.int32)
        energy.append(E_LOW + E_SPAN * fine.astype(jnp.float32) / (FINE * POINTS))
    level = jnp.where(
        odd, jnp.full((8, 128), levels[1], jnp.int32), jnp.full((8, 128), levels[0], jnp.int32)
    )
    potential = STEP_V * level.astype(jnp.float32)
    for t in range(SLABS):
        modes = jnp.concatenate(
            [jnp.broadcast_to(mode[4 * t + q : 4 * t + q + 1, :], (2, 128)) for q in range(4)], axis=0
        )
        re = [energy[i] - modes - potential - scat[0, i, 8 * t : 8 * t + 8, :] for i in range(2)]
        im = [ETA - scat[1, i, 8 * t : 8 * t + 8, :] for i in range(2)]
        a_out[t, 0, 0], a_out[t, 0, 1] = interleave(re[0], re[1], odd)
        a_out[t, 1, 0], a_out[t, 1, 1] = interleave(im[0], im[1], odd)
    en_out[0:1, :] = energy[0][0:1, :]
    en_out[1:2, :] = energy[1][0:1, :]
    own_energy = jnp.where(odd, energy[1], energy[0])
    own_occ = 1.0 / (1.0 + jnp.exp(own_energy / KT))

    targets = BLOCKS - jnp.where(s == yhi, 1, 0)
    pl.semaphore_wait(barrier, ENERGY - 1 + SLABS - 1 + targets)

    slab_copies = []
    for i in range(1, SLABS):
        peer = lax.rem(s + i, SLABS)
        copy = pltpu.make_async_remote_copy(
            src_ref=a_out.at[peer], dst_ref=a_in.at[s],
            send_sem=slab_send.at[i], recv_sem=slab_recv.at[i],
            device_id=peer * ENERGY + e, device_id_type=LOGICAL,
        )
        copy.start()
        slab_copies.append(copy)
    a_in[s] = a_out[s]

    def send_energy(i, carry):
        peer = lax.rem(e + i, ENERGY)
        pltpu.make_async_remote_copy(
            src_ref=en_out, dst_ref=en_in.at[e], send_sem=en_send, recv_sem=en_recv,
            device_id=s * ENERGY + peer, device_id_type=LOGICAL,
        ).start()
        return carry

    lax.fori_loop(1, ENERGY, send_energy, 0)
    en_in[e] = en_out[...]

    for copy in slab_copies:
        copy.wait_recv()

    a = [(a_in[layer // 2, 0, layer % 2], a_in[layer // 2, 1, layer % 2]) for layer in range(LAYERS)]
    contact = (jnp.zeros((8, 128), jnp.float32), jnp.full((8, 128), -GAMMA, jnp.float32))
    left, right = {}, {}
    g = contact
    for layer in range(LAYERS):
        left[layer] = g
        g = invert(a[layer][0] - g[0], a[layer][1] - g[1])
    g = contact
    for layer in reversed(range(LAYERS)):
        right[layer] = g
        g = invert(a[layer][0] - g[0], a[layer][1] - g[1])
    spectral = []
    for layer in range(LAYERS):
        g = invert(
            a[layer][0] - left[layer][0] - right[layer][0],
            a[layer][1] - left[layer][1] - right[layer][1],
        )
        spectral.append(-2.0 * g[1])
    for layer in range(LAYERS):
        for q in range(4):
            spec[4 * layer + q] = spectral[layer][2 * q : 2 * q + 2, :]

    def send_spec(i, carry):
        peer = lax.rem(e + i, ENERGY)
        pltpu.make_async_remote_copy(
            src_ref=spec.at[peer // ROW], dst_ref=spec_in.at[e], send_sem=spec_send, recv_sem=spec_recv,
            device_id=s * ENERGY + peer, device_id_type=LOGICAL,
        ).start()
        return carry

    lax.fori_loop(1, ENERGY, send_spec, 0)
    spec_in[e] = spec[r]

    for t in range(SLABS):
        first, second = interleave(own_occ * spectral[2 * t], own_occ * spectral[2 * t + 1], odd)
        dens_out[t, 0] = first
        dens_out[t, 1] = second
    dens_copies = []
    for i in range(1, SLABS):
        peer = lax.rem(s + i, SLABS)
        copy = pltpu.make_async_remote_copy(
            src_ref=dens_out.at[peer], dst_ref=dens_ref.at[:, s],
            send_sem=dens_send.at[i], recv_sem=dens_recv.at[i],
            device_id=peer * ENERGY + e, device_id_type=LOGICAL,
        )
        copy.start()
        dens_copies.append(copy)
    dens_ref[:, s] = dens_out[s]

    all_energies = pltpu.make_async_remote_copy(
        src_ref=en_in.at[pl.ds(0, ENERGY - 1)], dst_ref=en_in.at[pl.ds(0, ENERGY - 1)],
        send_sem=en_send, recv_sem=en_recv, device_id=me, device_id_type=LOGICAL,
    )
    all_energies.wait_recv()
    occ_all = 1.0 / (1.0 + jnp.exp(en_in[...].reshape(POINTS, 128) / KT))
    d_all[...] = occ_all

    all_spec = pltpu.make_async_remote_copy(
        src_ref=spec_in.at[pl.ds(0, ENERGY - 1)], dst_ref=spec_in.at[pl.ds(0, ENERGY - 1)],
        send_sem=spec_send, recv_sem=spec_recv, device_id=me, device_id_type=LOGICAL,
    )
    all_spec.wait_recv()
    spec_all = spec_in[...].reshape(POINTS, 128)
    occ_all = d_all[...]
    holes = (1.0 - occ_all) * spec_all
    h_all[0:POINTS, :] = holes
    h_all[POINTS : 2 * POINTS, :] = holes
    d_all[...] = occ_all * spec_all

    slot = (s * 4 + lax.rem(z, 4)) * 2 + z // 4

    def one_offset(i, carry):
        row = lax.rem(r + i, BLOCKS)
        start = POINTS - offsets[row * ROW + x]
        total = jnp.zeros((8, 128), jnp.float32)
        for t in range(POINTS // 8):
            total = total + d_all[8 * t : 8 * t + 8, :] * h_all[pl.ds(start + 8 * t, 8), :]
        pol_out[row] = jnp.sum(total, axis=0, keepdims=True) * (1.0 / POINTS)
        peer = yhi * ENERGY + row * ROW + x

        @pl.when(peer != me)
        def _():
            pltpu.make_async_remote_copy(
                src_ref=pol_out.at[row], dst_ref=pol_in.at[slot], send_sem=pol_send, recv_sem=pol_recv,
                device_id=peer, device_id_type=LOGICAL,
            ).start()

        return carry

    lax.fori_loop(0, BLOCKS, one_offset, 0)

    @pl.when(s == yhi)
    def _():
        pol_in[slot] = pol_out[r]

    def all_pol(count):
        return pltpu.make_async_remote_copy(
            src_ref=pol_in.at[pl.ds(0, count)], dst_ref=pol_in.at[pl.ds(0, count)],
            send_sem=pol_send, recv_sem=pol_recv, device_id=me, device_id_type=LOGICAL,
        )

    for copy in dens_copies:
        copy.wait()
    for copy in slab_copies:
        copy.wait_send()
    all_energies.wait_send()
    all_spec.wait_send()

    @pl.when(s == yhi)
    def _():
        all_pol(BLOCKS - 1).wait()

    @pl.when(s != yhi)
    def _():
        all_pol(BLOCKS).wait()

    for m in range(16):
        for k in range(2):
            pol_ref[m, k : k + 1, :] = pol_in[2 * m + k]


def local(mode_energy, levels, energy_jitter, offsets, scattering):
    modes = mode_energy.reshape(16, 128)
    scat = scattering.reshape(2, 2, 2, 16, 128).transpose(0, 1, 3, 2, 4).reshape(2, 2, 32, 128)
    f32 = jnp.float32
    dma = pltpu.SemaphoreType.DMA
    hbm = pl.BlockSpec(memory_space=pl.ANY)
    vmem = pl.BlockSpec(memory_space=pltpu.VMEM)
    density, polarization = pl.pallas_call(
        kernel,
        out_shape=(
            jax.ShapeDtypeStruct((2, SLABS, 8, 128), f32),
            jax.ShapeDtypeStruct((16, 2, 128), f32),
        ),
        in_specs=[hbm] * 5,
        out_specs=(vmem, vmem),
        scratch_shapes=[
            pltpu.VMEM((16, 128), f32),
            pltpu.SMEM((2,), jnp.int32),
            pltpu.SMEM((2,), jnp.int32),
            pltpu.SMEM((128,), jnp.int32),
            pltpu.VMEM((2, 2, 32, 128), f32),
            pltpu.VMEM((SLABS, 2, 2, 8, 128), f32),
            pltpu.VMEM((SLABS, 2, 2, 8, 128), f32),
            pltpu.VMEM((BLOCKS, 2, 128), f32),
            pltpu.VMEM((ENERGY, 2, 128), f32),
            pltpu.VMEM((2, 128), f32),
            pltpu.VMEM((ENERGY, 2, 128), f32),
            pltpu.VMEM((SLABS, 2, 8, 128), f32),
            pltpu.VMEM((POINTS, 128), f32),
            pltpu.VMEM((2 * POINTS, 128), f32),
            pltpu.VMEM((BLOCKS, 1, 128), f32),
            pltpu.VMEM((BLOCKS, 1, 128), f32),
            dma((2,)),
            dma((3,)),
            dma((SLABS,)),
            dma((SLABS,)),
            dma,
            dma,
            dma,
            dma,
            dma((SLABS,)),
            dma((SLABS,)),
            dma,
            dma,
        ],
        compiler_params=pltpu.CompilerParams(collective_id=0, has_side_effects=True),
        name="green_polarization",
    )(modes, levels, energy_jitter, offsets, scat)
    density = density.reshape(2, 16, 2, 128).transpose(0, 2, 1, 3).reshape(2, 2, 2048)
    polarization = polarization.transpose(1, 0, 2).reshape(1, 2, 2048)
    return density, polarization


def solution(mesh):
    placed = (P(), P("slab"), P("energy"), P(), P(None, "energy", "slab", None))
    return jax.shard_map(
        local,
        mesh=mesh,
        in_specs=placed,
        out_specs=(P("energy", "slab", None), P("energy", "slab", None)),
        check_vma=False,
    )
```

time: 108 us -> 43.4 us (0.40)
  Pallas kernels: 0 us -> 40 us
  local copies, waits for them, and re-layouts: 28.8 us -> 1.99 us
  waiting for transfers between devices: 24.4 us -> 0 us
  blocking collectives: 22.7 us -> 0 us
  starting transfers between devices: 20.9 us -> 0 us
  other arithmetic: 5.01 us -> 0 us
  matrix products: 4.27 us -> 0 us
    pallas_call x0 -> x1, Pallas kernels: none -> 40 us  [local(): pl.pallas_call(kernel, out_shape=(jax.ShapeDtypeStruct((2, SLABS, 8, 128)...]
    all_to_all x2 -> x0, waiting for transfers between devices: 24.4 us -> none  [the longest x1 12.3 us: local(): lax.all_to_all(stacked, 'energy', split_axis=3, concat_axis=0, tiled=True)]
    all_to_all x3 -> x0, blocking collectives: 22.7 us -> none  [the longest x2 15.7 us: moved_by_axis(): result = lax.all_to_all(result, axes[k], k, k, tiled=True)]
    all_to_all x2 -> x0, starting transfers between devices: 20.9 us -> none  [the longest x1 14.8 us: local(): lax.all_to_all(stacked, 'energy', split_axis=3, concat_axis=0, tiled=True)]
    unnamed x4, local copies, waits for them, and re-layouts: 14.6 us -> 1.99 us
    all_to_all x10 -> x0, local copies, waits for them, and re-layouts: 8.47 us -> none  [the longest x3 7.61 us: local(): lax.all_to_all(stacked, 'energy', split_axis=3, concat_axis=0, tiled=True)]
    another operation x2 -> x0, local copies, waits for them, and re-layouts: 4.4 us -> none  [the longest x1 4.4 us: local(): stacked = jnp.stack((density, hole_part), axis=1)]
    dot_general x4 -> x0, matrix products: 4.27 us -> none  [the longest x1 1.34 us: local(): jnp.dot(sin_table, flattened, precision=lax.Precision.HIGHEST)]
  transfers between devices with their start and end apart: 2 -> 0, of which waited for: 2 -> 0; matrix products, arithmetic and copies ran while one was open for 1% -> 0% of each run, Pallas kernels for 0% -> 0%
where the time goes in v1:
time: 43.4 us; the launch traced here: 42.7 us
  Pallas kernels  40 us (92%)
  local copies, waits for them, and re-layouts  1.99 us (5%)
  between operations  0.65 us (1%)
    pallas_call x1, Pallas kernels, local(): pl.pallas_call(kernel, out_shape=(jax.ShapeDtypeStruct((2, SLABS, 8, 128)...  40 us
    unnamed x4, local copies, waits for them, and re-layouts  1.99 us

profile of v1, /device:TPU:1, one launch (start us, length us, event | category | flops | bytes accessed | tf_op | source)
XLA Modules:
  0.0 42.7 jit_solution(14937541333689894208)
XLA Ops:
  0.6 40.0 %green_polarization.1 = (f32[2,4,8,128]{3,2,1,0:T(8,128)}, f32[16,2,128]{2,1,0:T(2,128)}) custom-call(f32[16,128]{1,0:T(8,128)} %bitcast.17, s32[2]{0:T(128)} %levels_hbm.1, s32[2]{0:T(128)} %jitter_hbm.1, s32[128]{0:T(128)} %offsets_hbm.1, f32[2,2,32,128]{3,2,1,0:T(8,128)} %bitcast.14), custom_call_target="tpu_custom_call" | custom-call | tf_op jit(solution)/shard_map/green_polarization/pallas_call | solution.py:268
  40.7 0.0 copy-start
  40.7 1.4 %copy.11 = f32[2,2,2048]{2,1,0:T(2,128)} copy(f32[2,2,2048]{2,1,0:T(2,128)} %bitcast.15) | data formatting | bytes 65536
  42.1 0.0 copy-done
  42.1 0.6 %copy.12 = f32[1,2,2048]{2,1,0:T(2,128)} copy(f32[1,2,2048]{2,1,0:T(2,128)S(1)} %bitcast.16) | data formatting | bytes 32768
Async XLA Ops:
  40.7 1.4 %copy-start = (f32[16,2,128]{2,1,0:T(2,128)S(1)}, f32[16,2,128]{2,1,0:T(2,128)}, u32[]{:S(2)}) copy-start(f32[16,2,128]{2,1,0:T(2,128)} %get-tuple-element.5) | copy-start | bytes 49156

commit v2 on v0

v2 whole, which is shorter than its diff:
```python
import jax
import jax.numpy as jnp
from jax import lax
from jax.experimental import pallas as pl
from jax.experimental.pallas import tpu as pltpu
from jax.sharding import PartitionSpec as P

FINE = 8
ETA = 0.1
GAMMA = 0.5
KT = 0.25
STEP_V = 0.15
E_LOW = -3.0
E_SPAN = 6.0

SLABS = 4
HUBS = 2
YS, ZS, XS = 4, 8, 4
ENERGY = YS * ZS * XS
ROWS = YS * ZS
POINTS = 256
LAYERS = 8
BLOCKS = 64
SENDERS = 32
LOGICAL = pl.DeviceIdType.LOGICAL


def invert(re, im):
    scale = 1.0 / (re * re + im * im)
    return re * scale, -im * scale


def interleave(first, second, odd):
    return (
        jnp.where(odd, pltpu.roll(second, 1, 0), first),
        jnp.where(odd, second, pltpu.roll(first, 7, 0)),
    )


def far_first(y, z, x):
    ys = [lax.rem(y + d, YS) * (ZS * XS) for d in range(YS)]
    zs = [lax.rem(z + d, ZS) * XS for d in range(ZS)]
    xs = [lax.rem(x + d, XS) for d in range(XS)]
    order = []
    for dy in range(YS):
        for dz in range(ZS):
            for dx in range(XS):
                hops = 2 * min(dy, YS - dy) + min(dz, ZS - dz) + min(dx, XS - dx)
                order.append((-hops, dy, dz, dx))
    order.sort()
    return [ys[dy] + zs[dz] + xs[dx] for hops, dy, dz, dx in order if hops]


def kernel(
    mode_hbm, levels_hbm, jitter_hbm, offsets_hbm, scat_hbm,
    dens_ref, pol_ref,
    mode, levels, jitter, offsets,
    raw_in, lev_out, lev_in, spec, spec_in, en_x, en_row, en_in, dens_out, d_all, h_all, pol_out, pol_in,
    go, load_sem, raw_send, raw_recv, lev_send, lev_recv, x_send, x_recv, en_send, en_recv,
    spec_send, spec_recv, dens_send, dens_recv, pol_send, pol_recv,
):
    s = lax.axis_index("slab")
    e = lax.axis_index("energy")
    y = e // (ZS * XS)
    z = lax.rem(e // XS, ZS)
    x = lax.rem(e, XS)
    me = s * ENERGY + e
    half = 2 * LAYERS

    barrier = pltpu.get_barrier_semaphore()
    level_load = pltpu.make_async_copy(levels_hbm, levels, load_sem.at[0])

    def remote(src, dst, send, recv, device):
        return pltpu.make_async_remote_copy(
            src_ref=src, dst_ref=dst, send_sem=send, recv_sem=recv, device_id=device, device_id_type=LOGICAL
        )

    def raw_copy(hub):
        return remote(
            scat_hbm.at[:, :, pl.ds(half * hub, half), :], raw_in.at[s],
            raw_send.at[hub], raw_recv.at[s], hub * ENERGY + e,
        )

    def lev_copy(hub):
        return remote(lev_out, lev_in.at[s], lev_send.at[hub], lev_recv.at[s], hub * ENERGY + e)

    def load_levels():
        level_load.wait()
        for i in range(2):
            level = jnp.full((1, 128), levels[i], jnp.int32)
            lev_out[i : i + 1, :] = STEP_V * level.astype(jnp.float32)

    def all_pol(count):
        return remote(pol_in.at[pl.ds(0, count)], pol_in.at[pl.ds(0, count)], pol_send, pol_recv, me)

    @pl.when(s >= HUBS)
    def _():
        level_load.start()
        pl.semaphore_wait(barrier, HUBS)
        for hub in range(HUBS):

            @pl.when(s == HUBS)
            def _():
                pl.semaphore_signal(go, 1, device_id=hub * ENERGY + e, device_id_type=LOGICAL)

        for hub in range(HUBS):
            raw_copy(hub).start()
        load_levels()
        for hub in range(HUBS):
            lev_copy(hub).start()
        for hub in range(HUBS):
            raw_copy(hub).wait_send()
            lev_copy(hub).wait_send()
            remote(
                dens_out.at[0], dens_ref.at[:, pl.ds(2 * hub, 2)],
                dens_send.at[0], dens_recv.at[hub], me,
            ).wait_recv()
        all_pol(SENDERS).wait_recv()

    @pl.when(s < HUBS)
    def _():
        other = HUBS - 1 - s
        for leaf in range(HUBS, SLABS):
            pl.semaphore_signal(barrier, 1, device_id=leaf * ENERGY + e, device_id_type=LOGICAL)
        peers = far_first(y, z, x)
        for peer in peers:
            pl.semaphore_signal(barrier, 1, device_id=s * ENERGY + peer, device_id_type=LOGICAL)

        loads = [
            pltpu.make_async_copy(jitter_hbm, jitter, load_sem.at[1]),
            pltpu.make_async_copy(mode_hbm.at[pl.ds(8 * s, 8)], mode, load_sem.at[2]),
            pltpu.make_async_copy(scat_hbm.at[:, :, pl.ds(half * s, half), :], raw_in.at[s], load_sem.at[3]),
            pltpu.make_async_copy(offsets_hbm, offsets, load_sem.at[4]),
        ]
        level_load.start()
        for copy in loads:
            copy.start()
        load_levels()
        lev_in[s] = lev_out[...]
        for copy in loads:
            copy.wait()

        odd = lax.rem(lax.broadcasted_iota(jnp.int32, (8, 128), 0), 2) == 1
        lane = lax.broadcasted_iota(jnp.int32, (8, 128), 1)
        energy = []
        for i in range(2):
            fine = jnp.full((8, 128), FINE * (2 * e + i) + jitter[i], jnp.int32)
            energy.append(E_LOW + E_SPAN * fine.astype(jnp.float32) / (FINE * POINTS))
        own_energy = jnp.where(odd, energy[1], energy[0])
        own_occ = 1.0 / (1.0 + jnp.exp(own_energy / KT))
        place = lane // 16
        mine = jnp.where(place == 2 * x, energy[0], jnp.where(place == 2 * x + 1, energy[1], 0.0))
        en_x[0] = mine[0:1, :]

        pl.semaphore_wait(go, 1)
        raw_copy(other).start()
        lev_copy(other).start()

        def wait_source(source):
            remote(raw_in.at[source], raw_in.at[source], raw_send.at[0], raw_recv.at[source], me).wait_recv()
            remote(lev_out, lev_in.at[source], lev_send.at[0], lev_recv.at[source], me).wait_recv()

        wait_source(other)
        for leaf in range(HUBS, SLABS):
            wait_source(leaf)

        for h in range(2):
            modes = [
                jnp.broadcast_to(mode[4 * h + q : 4 * h + q + 1, :], (2, 128)) for q in range(4)
            ]
            base = own_energy - jnp.concatenate(modes, axis=0)
            a = []
            for source in range(SLABS):
                part = [
                    interleave(
                        raw_in[source, c, 0, 8 * h : 8 * h + 8, :], raw_in[source, c, 1, 8 * h : 8 * h + 8, :], odd
                    )
                    for c in range(2)
                ]
                for k in range(2):
                    a.append((base - lev_in[source, k : k + 1, :] - part[0][k], ETA - part[1][k]))
            contact = (jnp.zeros((8, 128), jnp.float32), jnp.full((8, 128), -GAMMA, jnp.float32))
            left, right = {}, {}
            g = contact
            for layer in range(LAYERS):
                left[layer] = g
                g = invert(a[layer][0] - g[0], a[layer][1] - g[1])
            g = contact
            for layer in reversed(range(LAYERS)):
                right[layer] = g
                g = invert(a[layer][0] - g[0], a[layer][1] - g[1])
            density = []
            for layer in range(LAYERS):
                g = invert(
                    a[layer][0] - left[layer][0] - right[layer][0],
                    a[layer][1] - left[layer][1] - right[layer][1],
                )
                spectral = -2.0 * g[1]
                density.append(own_occ * spectral)
                for q in range(4):
                    spec[8 * layer + 4 * h + q] = spectral[2 * q : 2 * q + 2, :]
            for t in range(SLABS):
                first, second = interleave(density[2 * t], density[2 * t + 1], odd)
                dens_out[t, 0, h] = first
                dens_out[t, 1, h] = second

        pl.semaphore_wait(barrier, ENERGY - 1)
        for i in range(1, XS):
            remote(en_x.at[0], en_x.at[i], x_send, x_recv, me - x + lax.rem(x + i, XS)).start()

        for peer in peers:
            remote(
                spec.at[lax.rem(peer, BLOCKS)], spec_in.at[e], spec_send, spec_recv, s * ENERGY + peer
            ).start()
        block = lax.rem(e, BLOCKS)
        spec_in[e] = spec[block]

        def dens_copy(target):
            return remote(
                dens_out.at[target], dens_ref.at[:, pl.ds(2 * s, 2)],
                dens_send.at[target], dens_recv.at[s], target * ENERGY + e,
            )

        dens_copy(other).start()
        for leaf in range(HUBS, SLABS):
            dens_copy(leaf).start()
        dens_ref[:, pl.ds(2 * s, 2)] = dens_out[s]

        x_all = remote(en_x.at[pl.ds(1, XS - 1)], en_x.at[pl.ds(1, XS - 1)], x_send, x_recv, me)
        x_all.wait()
        en_row[...] = (en_x[0] + en_x[1]) + (en_x[2] + en_x[3])
        row = e // XS
        en_in[row] = en_row[...]
        for i in range(1, ROWS):
            peer = lax.rem(row + i, ROWS)
            remote(en_row, en_in.at[row], en_send, en_recv, s * ENERGY + peer * XS + x).start()
        en_all = remote(en_in.at[pl.ds(0, ROWS - 1)], en_in.at[pl.ds(0, ROWS - 1)], en_send, en_recv, me)
        en_all.wait()
        diagonal = place == lax.broadcasted_iota(jnp.int32, (8, 128), 0)
        for i in range(ROWS):
            spread = jnp.where(diagonal, jnp.broadcast_to(en_in[i], (8, 128)), -100.0)
            column = jnp.broadcast_to(jnp.max(spread, axis=1, keepdims=True), (8, 128))
            d_all[8 * i : 8 * i + 8, :] = 1.0 / (1.0 + jnp.exp(column / KT))

        spec_all = remote(
            spec_in.at[pl.ds(0, ENERGY - 1)], spec_in.at[pl.ds(0, ENERGY - 1)], spec_send, spec_recv, me
        )
        spec_all.wait()
        spectra = spec_in[...].reshape(POINTS, 128)
        occ = d_all[...]
        holes = (1.0 - occ) * spectra
        h_all[0:POINTS, :] = holes
        h_all[POINTS : 2 * POINTS, :] = holes
        d_all[...] = occ * spectra
        d = [d_all[8 * t : 8 * t + 8, :] for t in range(POINTS // 8)]

        first_offset = e - block
        layer = block // 8
        target = layer // 2
        slot = (s * 8 + lax.rem(block, 8)) * 2 + lax.rem(layer, 2)
        own = (target == s).astype(jnp.int32)

        def one_offset(i, carry):
            k = lax.rem(block + 1 + i, BLOCKS)
            start = POINTS - offsets[first_offset + k]
            parts = []
            for t in range(POINTS // 8):
                term = d[t] * h_all[pl.ds(start + 8 * t, 8), :]
                if t < 4:
                    parts.append(term)
                else:
                    parts[t % 4] = parts[t % 4] + term
            total = (parts[0] + parts[1]) + (parts[2] + parts[3])
            pol_out[k] = jnp.sum(total, axis=0, keepdims=True) * (1.0 / POINTS)
            peer = target * ENERGY + first_offset + k

            @pl.when(peer != me)
            def _():
                remote(pol_out.at[k], pol_in.at[slot], pol_send, pol_recv, peer).start()

            return carry

        lax.fori_loop(0, BLOCKS, one_offset, 0)

        @pl.when(own == 1)
        def _():
            pol_in[slot] = pol_out[block]
            remote(
                pol_out.at[pl.ds(0, BLOCKS - 1)], pol_out.at[pl.ds(0, BLOCKS - 1)], pol_send, pol_recv, me
            ).wait_send()
            all_pol(SENDERS - 1).wait_recv()

        @pl.when(own == 0)
        def _():
            remote(pol_out, pol_out, pol_send, pol_recv, me).wait_send()
            all_pol(SENDERS).wait_recv()

        dens_copy(other).wait_send()
        for leaf in range(HUBS, SLABS):
            dens_copy(leaf).wait_send()
        remote(
            dens_out.at[0], dens_ref.at[:, pl.ds(2 * other, 2)], dens_send.at[0], dens_recv.at[other], me
        ).wait_recv()
        raw_copy(other).wait_send()
        lev_copy(other).wait_send()

    for m in range(16):
        for k in range(2):
            pol_ref[m, k : k + 1, :] = pol_in[2 * m + k]


def local(mode_energy, levels, energy_jitter, offsets, scattering):
    modes = mode_energy.reshape(16, 128)
    scat = scattering.reshape(2, 2, 2, 16, 128).transpose(0, 1, 3, 2, 4).reshape(2, 2, 32, 128)
    f32 = jnp.float32
    dma = pltpu.SemaphoreType.DMA
    hbm = pl.BlockSpec(memory_space=pl.ANY)
    vmem = pl.BlockSpec(memory_space=pltpu.VMEM)
    density, polarization = pl.pallas_call(
        kernel,
        out_shape=(
            pltpu.VMEM((2, SLABS, 8, 128), f32),
            pltpu.VMEM((16, 2, 128), f32),
        ),
        in_specs=[hbm] * 5,
        out_specs=(vmem, vmem),
        scratch_shapes=[
            pltpu.VMEM((8, 128), f32),
            pltpu.SMEM((2,), jnp.int32),
            pltpu.SMEM((2,), jnp.int32),
            pltpu.SMEM((128,), jnp.int32),
            pltpu.VMEM((SLABS, 2, 2, 16, 128), f32),
            pltpu.VMEM((2, 128), f32),
            pltpu.VMEM((SLABS, 2, 128), f32),
            pltpu.VMEM((BLOCKS, 2, 128), f32),
            pltpu.VMEM((ENERGY, 2, 128), f32),
            pltpu.VMEM((XS, 1, 128), f32),
            pltpu.VMEM((1, 128), f32),
            pltpu.VMEM((ROWS, 1, 128), f32),
            pltpu.VMEM((SLABS, 2, 2, 8, 128), f32),
            pltpu.VMEM((POINTS, 128), f32),
            pltpu.VMEM((2 * POINTS, 128), f32),
            pltpu.VMEM((BLOCKS, 1, 128), f32),
            pltpu.VMEM((SENDERS, 1, 128), f32),
            pltpu.SemaphoreType.REGULAR,
            dma((5,)),
            dma((HUBS,)),
            dma((SLABS,)),
            dma((HUBS,)),
            dma((SLABS,)),
            dma,
            dma,
            dma,
            dma,
            dma,
            dma,
            dma((SLABS,)),
            dma((HUBS,)),
            dma,
            dma,
        ],
        compiler_params=pltpu.CompilerParams(collective_id=0, has_side_effects=True),
        name="green_polarization",
    )(modes, levels, energy_jitter, offsets, scat)
    density = density.reshape(2, 16, 2, 128).transpose(0, 2, 1, 3).reshape(2, 2, 2048)
    polarization = polarization.transpose(1, 0, 2).reshape(1, 2, 2048)
    return density, polarization


def solution(mesh):
    placed = (P(), P("slab"), P("energy"), P(), P(None, "energy", "slab", None))
    return jax.shard_map(
        local,
        mesh=mesh,
        in_specs=placed,
        out_specs=(P("energy", "slab", None), P("energy", "slab", None)),
        check_vma=False,
    )
```

time: 108 us -> 37.2 us (0.34)
  Pallas kernels: 0 us -> 35.2 us
  local copies, waits for them, and re-layouts: 28.8 us -> 1.22 us
  waiting for transfers between devices: 24.4 us -> 0 us
  blocking collectives: 22.7 us -> 0 us
  starting transfers between devices: 20.9 us -> 0 us
  other arithmetic: 5.01 us -> 0 us
  matrix products: 4.27 us -> 0 us
    pallas_call x0 -> x1, Pallas kernels: none -> 35.2 us  [local(): pl.pallas_call(kernel, out_shape=(pltpu.VMEM((2, SLABS, 8, 128), f32), pl...]
    all_to_all x2 -> x0, waiting for transfers between devices: 24.4 us -> none  [the longest x1 12.3 us: local(): lax.all_to_all(stacked, 'energy', split_axis=3, concat_axis=0, tiled=True)]
    all_to_all x3 -> x0, blocking collectives: 22.7 us -> none  [the longest x2 15.7 us: moved_by_axis(): result = lax.all_to_all(result, axes[k], k, k, tiled=True)]
    all_to_all x2 -> x0, starting transfers between devices: 20.9 us -> none  [the longest x1 14.8 us: local(): lax.all_to_all(stacked, 'energy', split_axis=3, concat_axis=0, tiled=True)]
    unnamed x4 -> x2, local copies, waits for them, and re-layouts: 14.6 us -> 1.22 us
    all_to_all x10 -> x0, local copies, waits for them, and re-layouts: 8.47 us -> none  [the longest x3 7.61 us: local(): lax.all_to_all(stacked, 'energy', split_axis=3, concat_axis=0, tiled=True)]
    another operation x2 -> x0, local copies, waits for them, and re-layouts: 4.4 us -> none  [the longest x1 4.4 us: local(): stacked = jnp.stack((density, hole_part), axis=1)]
    dot_general x4 -> x0, matrix products: 4.27 us -> none  [the longest x1 1.34 us: local(): jnp.dot(sin_table, flattened, precision=lax.Precision.HIGHEST)]
  transfers between devices with their start and end apart: 2 -> 0, of which waited for: 2 -> 0; matrix products, arithmetic and copies ran while one was open for 1% -> 0% of each run, Pallas kernels for 0% -> 0%
where the time goes in v2:
time: 37.2 us; the launch traced here: 37 us
  Pallas kernels  35.2 us (95%)
  local copies, waits for them, and re-layouts  1.22 us (3%)
  between operations  0.64 us (2%)
    pallas_call x1, Pallas kernels, local(): pl.pallas_call(kernel, out_shape=(pltpu.VMEM((2, SLABS, 8, 128), f32), pl...  35.2 us
    unnamed x2, local copies, waits for them, and re-layouts  1.22 us

profile of v2, /device:TPU:1, one launch (start us, length us, event | category | flops | bytes accessed | tf_op | source)
XLA Modules:
  0.0 37.0 jit_solution(667567541110887998)
XLA Ops:
  0.6 35.2 %green_polarization.1 = (f32[2,4,8,128]{3,2,1,0:T(8,128)S(1)}, f32[16,2,128]{2,1,0:T(2,128)S(1)}) custom-call(f32[16,128]{1,0:T(8,128)} %bitcast.17, s32[2]{0:T(128)} %levels_hbm.1, s32[2]{0:T(128)} %jitter_hbm.1, s32[128]{0:T(128)} %offsets_hbm.1, f32[2,2,32,128]{3,2,1,0:T(8,128)} %bitcast.16), custom_call_target="tpu_custom_call" | custom-call | tf_op jit(solution)/shard_map/green_polarization/pallas_call | solution.py:319
  35.8 0.6 %copy.11 = f32[2,2,2048]{2,1,0:T(2,128)} copy(f32[2,2,2048]{2,1,0:T(2,128)S(1)} %bitcast.14) | data formatting | bytes 65536
  36.4 0.6 %copy.12 = f32[1,2,2048]{2,1,0:T(2,128)} copy(f32[1,2,2048]{2,1,0:T(2,128)S(1)} %bitcast.15) | data formatting | bytes 32768

commit v3 on v2

--- a/solution.py
+++ b/solution.py
@@ -25,9 +25,13 @@
 LOGICAL = pl.DeviceIdType.LOGICAL
 
 
-def invert(re, im):
-    scale = 1.0 / (re * re + im * im)
-    return re * scale, -im * scale
+def times(p, q):
+    return p[0] * q[0] - p[1] * q[1], p[0] * q[1] + p[1] * q[0]
+
+
+def step(a, near, far):
+    product = times(a, near)
+    return product[0] - far[0], product[1] - far[1]
 
 
 def interleave(first, second, odd):
@@ -37,18 +41,34 @@
     )
 
 
+def hops_of(dy, dz, dx):
+    return 2 * min(dy, YS - dy) + min(dz, ZS - dz) + min(dx, XS - dx)
+
+
 def far_first(y, z, x):
     ys = [lax.rem(y + d, YS) * (ZS * XS) for d in range(YS)]
     zs = [lax.rem(z + d, ZS) * XS for d in range(ZS)]
     xs = [lax.rem(x + d, XS) for d in range(XS)]
-    order = []
-    for dy in range(YS):
-        for dz in range(ZS):
-            for dx in range(XS):
-                hops = 2 * min(dy, YS - dy) + min(dz, ZS - dz) + min(dx, XS - dx)
-                order.append((-hops, dy, dz, dx))
-    order.sort()
+    order = sorted(
+        (-hops_of(dy, dz, dx), dy, dz, dx) for dy in range(YS) for dz in range(ZS) for dx in range(XS)
+    )
     return [ys[dy] + zs[dz] + xs[dx] for hops, dy, dz, dx in order if hops]
+
+
+def far_first_of(y, z, x, parity):
+    ys = [lax.rem(y + d, YS) * (ZS * XS) for d in range(YS)]
+    xs = [lax.rem(x + d, XS) for d in range(XS)]
+    same = lax.rem(z, 2) == parity
+    steps = ((4, 3), (2, 5), (6, 1), (0, 7))
+    zs = [lax.rem(z + jnp.where(same, even, odd), ZS) * XS for even, odd in steps]
+    order = sorted(
+        (-hops_of(dy, even, dx) - hops_of(dy, odd, dx), dy, n, dx)
+        for dy in range(YS)
+        for n, (even, odd) in enumerate(steps)
+        for dx in range(XS)
+    )
+    assert order[-1][1:] == (0, 3, 0)
+    return [ys[dy] + zs[n] + xs[dx] for hops, dy, n, dx in order]
 
 
 def kernel(
@@ -65,7 +85,7 @@
     z = lax.rem(e // XS, ZS)
     x = lax.rem(e, XS)
     me = s * ENERGY + e
-    half = 2 * LAYERS
+    half = 16
 
     barrier = pltpu.get_barrier_semaphore()
     level_load = pltpu.make_async_copy(levels_hbm, levels, load_sem.at[0])
@@ -75,10 +95,10 @@
             src_ref=src, dst_ref=dst, send_sem=send, recv_sem=recv, device_id=device, device_id_type=LOGICAL
         )
 
-    def raw_copy(hub):
+    def raw_copy(hub, h):
         return remote(
-            scat_hbm.at[:, :, pl.ds(half * hub, half), :], raw_in.at[s],
-            raw_send.at[hub], raw_recv.at[s], hub * ENERGY + e,
+            scat_hbm.at[:, :, pl.ds(half * hub + 8 * h, 8), :], raw_in.at[s, h],
+            raw_send.at[hub, h], raw_recv.at[s, h], hub * ENERGY + e,
         )
 
     def lev_copy(hub):
@@ -103,13 +123,15 @@
             def _():
                 pl.semaphore_signal(go, 1, device_id=hub * ENERGY + e, device_id_type=LOGICAL)
 
-        for hub in range(HUBS):
-            raw_copy(hub).start()
+        for h in range(2):
+            for hub in range(HUBS):
+                raw_copy(hub, h).start()
         load_levels()
         for hub in range(HUBS):
             lev_copy(hub).start()
         for hub in range(HUBS):
-            raw_copy(hub).wait_send()
+            for h in range(2):
+                raw_copy(hub, h).wait_send()
             lev_copy(hub).wait_send()
             remote(
                 dens_out.at[0], dens_ref.at[:, pl.ds(2 * hub, 2)],
@@ -129,8 +151,12 @@
         loads = [
             pltpu.make_async_copy(jitter_hbm, jitter, load_sem.at[1]),
             pltpu.make_async_copy(mode_hbm.at[pl.ds(8 * s, 8)], mode, load_sem.at[2]),
-            pltpu.make_async_copy(scat_hbm.at[:, :, pl.ds(half * s, half), :], raw_in.at[s], load_sem.at[3]),
-            pltpu.make_async_copy(offsets_hbm, offsets, load_sem.at[4]),
+            pltpu.make_async_copy(offsets_hbm, offsets, load_sem.at[3]),
+        ] + [
+            pltpu.make_async_copy(
+                scat_hbm.at[:, :, pl.ds(half * s + 8 * h, 8), :], raw_in.at[s, h], load_sem.at[4 + h]
+            )
+            for h in range(2)
         ]
         level_load.start()
         for copy in loads:
@@ -153,66 +179,94 @@
         en_x[0] = mine[0:1, :]
 
         pl.semaphore_wait(go, 1)
-        raw_copy(other).start()
+        for h in range(2):
+            raw_copy(other, h).start()
         lev_copy(other).start()
 
-        def wait_source(source):
-            remote(raw_in.at[source], raw_in.at[source], raw_send.at[0], raw_recv.at[source], me).wait_recv()
-            remote(lev_out, lev_in.at[source], lev_send.at[0], lev_recv.at[source], me).wait_recv()
-
-        wait_source(other)
-        for leaf in range(HUBS, SLABS):
-            wait_source(leaf)
-
+        base = []
         for h in range(2):
             modes = [
                 jnp.broadcast_to(mode[4 * h + q : 4 * h + q + 1, :], (2, 128)) for q in range(4)
             ]
-            base = own_energy - jnp.concatenate(modes, axis=0)
-            a = []
-            for source in range(SLABS):
-                part = [
-                    interleave(
-                        raw_in[source, c, 0, 8 * h : 8 * h + 8, :], raw_in[source, c, 1, 8 * h : 8 * h + 8, :], odd
-                    )
-                    for c in range(2)
-                ]
-                for k in range(2):
-                    a.append((base - lev_in[source, k : k + 1, :] - part[0][k], ETA - part[1][k]))
-            contact = (jnp.zeros((8, 128), jnp.float32), jnp.full((8, 128), -GAMMA, jnp.float32))
-            left, right = {}, {}
-            g = contact
-            for layer in range(LAYERS):
-                left[layer] = g
-                g = invert(a[layer][0] - g[0], a[layer][1] - g[1])
-            g = contact
-            for layer in reversed(range(LAYERS)):
-                right[layer] = g
-                g = invert(a[layer][0] - g[0], a[layer][1] - g[1])
+            base.append(own_energy - jnp.concatenate(modes, axis=0))
+
+        def wait_levels(source):
+            remote(lev_out, lev_in.at[source], lev_send.at[0], lev_recv.at[source], me).wait_recv()
+
+        def wait_raw(source, h):
+            remote(
+                raw_in.at[source, h], raw_in.at[source, h], raw_send.at[0, 0], raw_recv.at[source, h], me
+            ).wait_recv()
+
+        def coefficients(source, h):
+            part = [interleave(raw_in[source, h, c, 0], raw_in[source, h, c, 1], odd) for c in range(2)]
+            return [
+                (base[h] - lev_in[source, k : k + 1, :] - part[0][k], ETA - part[1][k]) for k in range(2)
+            ]
+
+        wait_levels(other)
+        one = jnp.full((8, 128), 1.0, jnp.float32)
+        zero = jnp.zeros((8, 128), jnp.float32)
+        contact = (zero, jnp.full((8, 128), -GAMMA, jnp.float32))
+        early, theta = [], []
+        for h in range(2):
+            wait_raw(other, h)
+            a = coefficients(0, h) + coefficients(1, h)
+            chain = [contact, (one, zero), (a[0][0], a[0][1] + GAMMA)]
+            for layer in range(1, 4):
+                chain.append(step(a[layer], chain[-1], chain[-2]))
+            early.append(a)
+            theta.append(chain[1:])
+
+        block = lax.rem(e, BLOCKS)
+        for h in range(2):
+            for leaf in range(HUBS, SLABS):
+                if h == 0:
+                    wait_levels(leaf)
+                wait_raw(leaf, h)
+            a = early[h] + coefficients(2, h) + coefficients(3, h)
+            left = list(theta[h])
+            for layer in range(4, LAYERS - 1):
+                left.append(step(a[layer], left[-1], left[-2]))
+            right = [(one, zero), (a[LAYERS - 1][0], a[LAYERS - 1][1] + GAMMA)]
+            for layer in reversed(range(1, LAYERS - 1)):
+                right.append(step(a[layer], right[-1], right[-2]))
+            det = step(a[4], times(left[4], right[3]), times(left[3], right[3]))
+            tail = times(left[4], right[2])
+            det = (det[0] - tail[0], det[1] - tail[1])
+            scale = 2.0 / (det[0] * det[0] + det[1] * det[1])
+            weight = (-det[0] * scale, det[1] * scale)
             density = []
             for layer in range(LAYERS):
-                g = invert(
-                    a[layer][0] - left[layer][0] - right[layer][0],
-                    a[layer][1] - left[layer][1] - right[layer][1],
-                )
-                spectral = -2.0 * g[1]
+                product = times(left[layer], right[LAYERS - 1 - layer])
+                spectral = product[0] * weight[1] + product[1] * weight[0]
                 density.append(own_occ * spectral)
                 for q in range(4):
                     spec[8 * layer + 4 * h + q] = spectral[2 * q : 2 * q + 2, :]
+
+            if h == 0:
+                pl.semaphore_wait(barrier, ENERGY - 1)
+                for i in range(1, XS):
+                    remote(en_x.at[0], en_x.at[i], x_send, x_recv, me - x + lax.rem(x + i, XS)).start()
+
+            def send_spec(peer):
+                remote(
+                    spec.at[lax.rem(peer, BLOCKS)], spec_in.at[e], spec_send, spec_recv, s * ENERGY + peer
+                ).start()
+
+            group = far_first_of(y, z, x, h)
+            for peer in group[:-1]:
+                send_spec(peer)
+            nearest = group[-1]
+
+            @pl.when(nearest != e)
+            def _():
+                send_spec(nearest)
+
             for t in range(SLABS):
                 first, second = interleave(density[2 * t], density[2 * t + 1], odd)
                 dens_out[t, 0, h] = first
                 dens_out[t, 1, h] = second
-
-        pl.semaphore_wait(barrier, ENERGY - 1)
-        for i in range(1, XS):
-            remote(en_x.at[0], en_x.at[i], x_send, x_recv, me - x + lax.rem(x + i, XS)).start()
-
-        for peer in peers:
-            remote(
-                spec.at[lax.rem(peer, BLOCKS)], spec_in.at[e], spec_send, spec_recv, s * ENERGY + peer
-            ).start()
-        block = lax.rem(e, BLOCKS)
         spec_in[e] = spec[block]
 
         def dens_copy(target):
@@ -255,13 +309,18 @@
         d = [d_all[8 * t : 8 * t + 8, :] for t in range(POINTS // 8)]
 
         first_offset = e - block
+        high = lax.rem(y, 2)
         layer = block // 8
         target = layer // 2
         slot = (s * 8 + lax.rem(block, 8)) * 2 + lax.rem(layer, 2)
         own = (target == s).astype(jnp.int32)
 
         def one_offset(i, carry):
-            k = lax.rem(block + 1 + i, BLOCKS)
+            n = i // 8
+            dz = 4 + jnp.where(lax.rem(n, 2) == 1, -((n + 1) // 2), n // 2)
+            to_x = lax.rem(x + 2 + lax.rem(i, 4), XS)
+            to_y = lax.rem(high + 1 + lax.rem(i, 8) // 4, 2)
+            k = to_y * (ZS * XS) + lax.rem(z + dz, ZS) * XS + to_x
             start = POINTS - offsets[first_offset + k]
             parts = []
             for t in range(POINTS // 8):
@@ -301,12 +360,24 @@
         remote(
             dens_out.at[0], dens_ref.at[:, pl.ds(2 * other, 2)], dens_send.at[0], dens_recv.at[other], me
         ).wait_recv()
-        raw_copy(other).wait_send()
+        for h in range(2):
+            raw_copy(other, h).wait_send()
         lev_copy(other).wait_send()
 
     for m in range(16):
         for k in range(2):
             pol_ref[m, k : k + 1, :] = pol_in[2 * m + k]
+
+
+def write_out(dens_ref, pol_ref, dens_hbm, pol_hbm, sem):
+    copies = [
+        pltpu.make_async_copy(dens_ref, dens_hbm, sem.at[0]),
+        pltpu.make_async_copy(pol_ref, pol_hbm, sem.at[1]),
+    ]
+    for copy in copies:
+        copy.start()
+    for copy in copies:
+        copy.wait()
 
 
 def local(mode_energy, levels, energy_jitter, offsets, scattering):
@@ -329,7 +400,7 @@
             pltpu.SMEM((2,), jnp.int32),
             pltpu.SMEM((2,), jnp.int32),
             pltpu.SMEM((128,), jnp.int32),
-            pltpu.VMEM((SLABS, 2, 2, 16, 128), f32),
+            pltpu.VMEM((SLABS, 2, 2, 2, 8, 128), f32),
             pltpu.VMEM((2, 128), f32),
             pltpu.VMEM((SLABS, 2, 128), f32),
             pltpu.VMEM((BLOCKS, 2, 128), f32),
@@ -343,9 +414,9 @@
             pltpu.VMEM((BLOCKS, 1, 128), f32),
             pltpu.VMEM((SENDERS, 1, 128), f32),
             pltpu.SemaphoreType.REGULAR,
-            dma((5,)),
-            dma((HUBS,)),
-            dma((SLABS,)),
+            dma((6,)),
+            dma((HUBS, 2)),
+            dma((SLABS, 2)),
             dma((HUBS,)),
             dma((SLABS,)),
             dma,
@@ -362,6 +433,20 @@
         compiler_params=pltpu.CompilerParams(collective_id=0, has_side_effects=True),
         name="green_polarization",
     )(modes, levels, energy_jitter, offsets, scat)
+    density, polarization = pl.pallas_call(
+        write_out,
+        out_shape=(
+            jax.ShapeDtypeStruct((2, SLABS, 8, 128), f32),
+            jax.ShapeDtypeStruct((16, 2, 128), f32),
+        ),
+        in_specs=[vmem] * 2,
+        out_specs=(hbm, hbm),
+        scratch_shapes=[dma((2,))],
+        name="write_out",
+    )(
+        pltpu.with_memory_space_constraint(density, pltpu.VMEM),
+        pltpu.with_memory_space_constraint(polarization, pltpu.VMEM),
+    )
     density = density.reshape(2, 16, 2, 128).transpose(0, 2, 1, 3).reshape(2, 2, 2048)
     polarization = polarization.transpose(1, 0, 2).reshape(1, 2, 2048)
     return density, polarization

time: 37.2 us -> 37 us (level)
  local copies, waits for them, and re-layouts: 1.22 us -> 0 us
  Pallas kernels: 35.2 us -> 36.1 us
    unnamed x2 -> x0, local copies, waits for them, and re-layouts: 1.22 us -> none
    pallas_call x0 -> x1, Pallas kernels: none -> 0.64 us  [local(): pl.pallas_call(write_out, out_shape=(jax.ShapeDtypeStruct((2, SLABS, 8, 1...]
where the time goes in v3:
time: 37 us; the launch traced here: 36.8 us
  Pallas kernels  36.1 us (98%)
  between operations  0.64 us (2%)
    pallas_call x1, Pallas kernels, local(): pl.pallas_call(kernel, out_shape=(pltpu.VMEM((2, SLABS, 8, 128), f32), pl...  35.5 us

profile of v3, /device:TPU:1, one launch (start us, length us, event | category | flops | bytes accessed | tf_op | source)
XLA Modules:
  0.0 36.8 jit_solution(10618758873150770729)
XLA Ops:
  0.6 35.5 %green_polarization.1 = (f32[2,4,8,128]{3,2,1,0:T(8,128)S(1)}, f32[16,2,128]{2,1,0:T(2,128)S(1)}) custom-call(f32[16,128]{1,0:T(8,128)} %bitcast.15, s32[2]{0:T(128)} %levels_hbm.1, s32[2]{0:T(128)} %jitter_hbm.1, s32[128]{0:T(128)} %offsets_hbm.1, f32[2,2,32,128]{3,2,1,0:T(8,128)} %bitcast.14), custom_call_target="tpu_custom_call" | custom-call | tf_op jit(solution)/shard_map/green_polarization/pallas_call | solution.py:390
  36.1 0.6 %write_out.1 = (f32[2,4,8,128]{3,2,1,0:T(8,128)}, f32[16,2,128]{2,1,0:T(2,128)}) custom-call(f32[2,4,8,128]{3,2,1,0:T(8,128)S(1)} %get-tuple-element.6.dens_ref, f32[16,2,128]{2,1,0:T(2,128)S(1)} %get-tuple-element.7.pol_ref), custom_call_target="tpu_custom_call" | custom-call | tf_op jit(solution)/shard_map/write_out/pallas_call | solution.py:436

commit v4 on v3

--- a/solution.py
+++ b/solution.py
@@ -75,8 +75,8 @@
     mode_hbm, levels_hbm, jitter_hbm, offsets_hbm, scat_hbm,
     dens_ref, pol_ref,
     mode, levels, jitter, offsets,
-    raw_in, lev_out, lev_in, spec, spec_in, en_x, en_row, en_in, dens_out, d_all, h_all, pol_out, pol_in,
-    go, load_sem, raw_send, raw_recv, lev_send, lev_recv, x_send, x_recv, en_send, en_recv,
+    raw_in, lev_out, lev_in, spec, spec_in, en_row, en_in, dens_out, d_all, h_all, pol_out, pol_in,
+    go, load_sem, raw_send, raw_recv, lev_send, lev_recv, en_send, en_recv,
     spec_send, spec_recv, dens_send, dens_recv, pol_send, pol_recv,
 ):
     s = lax.axis_index("slab")
@@ -176,7 +176,7 @@
         own_occ = 1.0 / (1.0 + jnp.exp(own_energy / KT))
         place = lane // 16
         mine = jnp.where(place == 2 * x, energy[0], jnp.where(place == 2 * x + 1, energy[1], 0.0))
-        en_x[0] = mine[0:1, :]
+        en_row[...] = mine[0:1, :]
 
         pl.semaphore_wait(go, 1)
         for h in range(2):
@@ -219,6 +219,18 @@
             theta.append(chain[1:])
 
         block = lax.rem(e, BLOCKS)
+        def send_energies():
+            for peer in peers:
+                remote(en_row, en_in.at[e], en_send, en_recv, s * ENERGY + peer).start()
+
+        pl.semaphore_wait(barrier, ENERGY - 1)
+
+        @pl.when(s == 0)
+        def _():
+            send_energies()
+
+        en_in[e] = en_row[...]
+
         for h in range(2):
             for leaf in range(HUBS, SLABS):
                 if h == 0:
@@ -244,10 +256,6 @@
                 for q in range(4):
                     spec[8 * layer + 4 * h + q] = spectral[2 * q : 2 * q + 2, :]
 
-            if h == 0:
-                pl.semaphore_wait(barrier, ENERGY - 1)
-                for i in range(1, XS):
-                    remote(en_x.at[0], en_x.at[i], x_send, x_recv, me - x + lax.rem(x + i, XS)).start()
 
             def send_spec(peer):
                 remote(
@@ -262,6 +270,12 @@
             @pl.when(nearest != e)
             def _():
                 send_spec(nearest)
+
+            if h == 1:
+
+                @pl.when(s == 1)
+                def _():
+                    send_energies()
 
             for t in range(SLABS):
                 first, second = interleave(density[2 * t], density[2 * t + 1], odd)
@@ -280,19 +294,12 @@
             dens_copy(leaf).start()
         dens_ref[:, pl.ds(2 * s, 2)] = dens_out[s]
 
-        x_all = remote(en_x.at[pl.ds(1, XS - 1)], en_x.at[pl.ds(1, XS - 1)], x_send, x_recv, me)
-        x_all.wait()
-        en_row[...] = (en_x[0] + en_x[1]) + (en_x[2] + en_x[3])
-        row = e // XS
-        en_in[row] = en_row[...]
-        for i in range(1, ROWS):
-            peer = lax.rem(row + i, ROWS)
-            remote(en_row, en_in.at[row], en_send, en_recv, s * ENERGY + peer * XS + x).start()
-        en_all = remote(en_in.at[pl.ds(0, ROWS - 1)], en_in.at[pl.ds(0, ROWS - 1)], en_send, en_recv, me)
+        en_all = remote(en_in.at[pl.ds(0, ENERGY - 1)], en_in.at[pl.ds(0, ENERGY - 1)], en_send, en_recv, me)
         en_all.wait()
         diagonal = place == lax.broadcasted_iota(jnp.int32, (8, 128), 0)
         for i in range(ROWS):
-            spread = jnp.where(diagonal, jnp.broadcast_to(en_in[i], (8, 128)), -100.0)
+            together = (en_in[4 * i] + en_in[4 * i + 1]) + (en_in[4 * i + 2] + en_in[4 * i + 3])
+            spread = jnp.where(diagonal, jnp.broadcast_to(together, (8, 128)), -100.0)
             column = jnp.broadcast_to(jnp.max(spread, axis=1, keepdims=True), (8, 128))
             d_all[8 * i : 8 * i + 8, :] = 1.0 / (1.0 + jnp.exp(column / KT))
 
@@ -315,12 +322,7 @@
         slot = (s * 8 + lax.rem(block, 8)) * 2 + lax.rem(layer, 2)
         own = (target == s).astype(jnp.int32)
 
-        def one_offset(i, carry):
-            n = i // 8
-            dz = 4 + jnp.where(lax.rem(n, 2) == 1, -((n + 1) // 2), n // 2)
-            to_x = lax.rem(x + 2 + lax.rem(i, 4), XS)
-            to_y = lax.rem(high + 1 + lax.rem(i, 8) // 4, 2)
-            k = to_y * (ZS * XS) + lax.rem(z + dz, ZS) * XS + to_x
+        def correlate(k):
             start = POINTS - offsets[first_offset + k]
             parts = []
             for t in range(POINTS // 8):
@@ -331,15 +333,23 @@
                     parts[t % 4] = parts[t % 4] + term
             total = (parts[0] + parts[1]) + (parts[2] + parts[3])
             pol_out[k] = jnp.sum(total, axis=0, keepdims=True) * (1.0 / POINTS)
+
+        def give(k):
             peer = target * ENERGY + first_offset + k
-
-            @pl.when(peer != me)
-            def _():
-                remote(pol_out.at[k], pol_in.at[slot], pol_send, pol_recv, peer).start()
-
+            remote(pol_out.at[k], pol_in.at[slot], pol_send, pol_recv, peer).start()
+
+        def one_offset(i, carry):
+            k = lax.rem(block + 1 + i, BLOCKS)
+            correlate(k)
+            give(k)
             return carry
 
-        lax.fori_loop(0, BLOCKS, one_offset, 0)
+        lax.fori_loop(0, BLOCKS - 1, one_offset, 0, unroll=3)
+        correlate(block)
+
+        @pl.when(own == 0)
+        def _():
+            give(block)
 
         @pl.when(own == 1)
         def _():
@@ -405,9 +415,8 @@
             pltpu.VMEM((SLABS, 2, 128), f32),
             pltpu.VMEM((BLOCKS, 2, 128), f32),
             pltpu.VMEM((ENERGY, 2, 128), f32),
-            pltpu.VMEM((XS, 1, 128), f32),
             pltpu.VMEM((1, 128), f32),
-            pltpu.VMEM((ROWS, 1, 128), f32),
+            pltpu.VMEM((ENERGY, 1, 128), f32),
             pltpu.VMEM((SLABS, 2, 2, 8, 128), f32),
             pltpu.VMEM((POINTS, 128), f32),
             pltpu.VMEM((2 * POINTS, 128), f32),
@@ -419,8 +428,6 @@
             dma((SLABS, 2)),
             dma((HUBS,)),
             dma((SLABS,)),
-            dma,
-            dma,
             dma,
             dma,
             dma,

time: 37 us -> 36.3 us (0.981)
  Pallas kernels: 36.1 us -> 35.4 us
    pallas_call x1, Pallas kernels: 35.5 us -> 34.8 us  [local(): pl.pallas_call(kernel, out_shape=(pltpu.VMEM((2, SLABS, 8, 128), f32), pl...]
where the time goes in v4:
time: 36.3 us; the launch traced here: 36.1 us
  Pallas kernels  35.4 us (98%)
  between operations  0.64 us (2%)
    pallas_call x1, Pallas kernels, local(): pl.pallas_call(kernel, out_shape=(pltpu.VMEM((2, SLABS, 8, 128), f32), pl...  34.8 us

profile of v4, /device:TPU:1, one launch (start us, length us, event | category | flops | bytes accessed | tf_op | source)
XLA Modules:
  0.0 36.1 jit_solution(12927698252227845708)
XLA Ops:
  0.6 34.8 %green_polarization.1 = (f32[2,4,8,128]{3,2,1,0:T(8,128)S(1)}, f32[16,2,128]{2,1,0:T(2,128)S(1)}) custom-call(f32[16,128]{1,0:T(8,128)} %bitcast.15, s32[2]{0:T(128)} %levels_hbm.1, s32[2]{0:T(128)} %jitter_hbm.1, s32[128]{0:T(128)} %offsets_hbm.1, f32[2,2,32,128]{3,2,1,0:T(8,128)} %bitcast.14), custom_call_target="tpu_custom_call" | custom-call | tf_op jit(solution)/shard_map/green_polarization/pallas_call | solution.py:400
  35.4 0.6 %write_out.1 = (f32[2,4,8,128]{3,2,1,0:T(8,128)}, f32[16,2,128]{2,1,0:T(2,128)}) custom-call(f32[2,4,8,128]{3,2,1,0:T(8,128)S(1)} %get-tuple-element.6.dens_ref, f32[16,2,128]{2,1,0:T(2,128)S(1)} %get-tuple-element.7.pol_ref), custom_call_target="tpu_custom_call" | custom-call | tf_op jit(solution)/shard_map/write_out/pallas_call | solution.py:443

commit v5 on v4

--- a/solution.py
+++ b/solution.py
@@ -75,8 +75,8 @@
     mode_hbm, levels_hbm, jitter_hbm, offsets_hbm, scat_hbm,
     dens_ref, pol_ref,
     mode, levels, jitter, offsets,
-    raw_in, lev_out, lev_in, spec, spec_in, en_row, en_in, dens_out, d_all, h_all, pol_out, pol_in,
-    go, load_sem, raw_send, raw_recv, lev_send, lev_recv, en_send, en_recv,
+    raw_in, lev_out, lev_in, spec, spec_in, en_row, en_in, occ_all, dens_out, d_all, h_all, pol_out, pol_in,
+    go, load_sem, raw_send, raw_recv, lev_send, lev_recv, en_send, en_recv, occ_send, occ_recv,
     spec_send, spec_recv, dens_send, dens_recv, pol_send, pol_recv,
 ):
     s = lax.axis_index("slab")
@@ -271,12 +271,6 @@
             def _():
                 send_spec(nearest)
 
-            if h == 1:
-
-                @pl.when(s == 1)
-                def _():
-                    send_energies()
-
             for t in range(SLABS):
                 first, second = interleave(density[2 * t], density[2 * t + 1], odd)
                 dens_out[t, 0, h] = first
@@ -294,21 +288,31 @@
             dens_copy(leaf).start()
         dens_ref[:, pl.ds(2 * s, 2)] = dens_out[s]
 
-        en_all = remote(en_in.at[pl.ds(0, ENERGY - 1)], en_in.at[pl.ds(0, ENERGY - 1)], en_send, en_recv, me)
-        en_all.wait()
-        diagonal = place == lax.broadcasted_iota(jnp.int32, (8, 128), 0)
-        for i in range(ROWS):
-            together = (en_in[4 * i] + en_in[4 * i + 1]) + (en_in[4 * i + 2] + en_in[4 * i + 3])
-            spread = jnp.where(diagonal, jnp.broadcast_to(together, (8, 128)), -100.0)
-            column = jnp.broadcast_to(jnp.max(spread, axis=1, keepdims=True), (8, 128))
-            d_all[8 * i : 8 * i + 8, :] = 1.0 / (1.0 + jnp.exp(column / KT))
+        occ_copy = remote(occ_all, occ_all, occ_send, occ_recv, other * ENERGY + e)
+
+        @pl.when(s == 0)
+        def _():
+            remote(
+                en_in.at[pl.ds(0, ENERGY - 1)], en_in.at[pl.ds(0, ENERGY - 1)], en_send, en_recv, me
+            ).wait()
+            diagonal = place == lax.broadcasted_iota(jnp.int32, (8, 128), 0)
+            for i in range(ROWS):
+                together = (en_in[4 * i] + en_in[4 * i + 1]) + (en_in[4 * i + 2] + en_in[4 * i + 3])
+                spread = jnp.where(diagonal, jnp.broadcast_to(together, (8, 128)), -100.0)
+                column = jnp.broadcast_to(jnp.max(spread, axis=1, keepdims=True), (8, 128))
+                occ_all[8 * i : 8 * i + 8, :] = 1.0 / (1.0 + jnp.exp(column / KT))
+            occ_copy.start()
+
+        @pl.when(s == 1)
+        def _():
+            occ_copy.wait_recv()
 
         spec_all = remote(
             spec_in.at[pl.ds(0, ENERGY - 1)], spec_in.at[pl.ds(0, ENERGY - 1)], spec_send, spec_recv, me
         )
         spec_all.wait()
         spectra = spec_in[...].reshape(POINTS, 128)
-        occ = d_all[...]
+        occ = occ_all[...]
         holes = (1.0 - occ) * spectra
         h_all[0:POINTS, :] = holes
         h_all[POINTS : 2 * POINTS, :] = holes
@@ -327,11 +331,11 @@
             parts = []
             for t in range(POINTS // 8):
                 term = d[t] * h_all[pl.ds(start + 8 * t, 8), :]
-                if t < 4:
+                if t < 2:
                     parts.append(term)
                 else:
-                    parts[t % 4] = parts[t % 4] + term
-            total = (parts[0] + parts[1]) + (parts[2] + parts[3])
+                    parts[t % 2] = parts[t % 2] + term
+            total = parts[0] + parts[1]
             pol_out[k] = jnp.sum(total, axis=0, keepdims=True) * (1.0 / POINTS)
 
         def give(k):
@@ -339,7 +343,7 @@
             remote(pol_out.at[k], pol_in.at[slot], pol_send, pol_recv, peer).start()
 
         def one_offset(i, carry):
-            k = lax.rem(block + 1 + i, BLOCKS)
+            k = lax.rem(block + BLOCKS - 1 - i, BLOCKS)
             correlate(k)
             give(k)
             return carry
@@ -363,6 +367,10 @@
         def _():
             remote(pol_out, pol_out, pol_send, pol_recv, me).wait_send()
             all_pol(SENDERS).wait_recv()
+
+        @pl.when(s == 0)
+        def _():
+            occ_copy.wait_send()
 
         dens_copy(other).wait_send()
         for leaf in range(HUBS, SLABS):
@@ -417,6 +425,7 @@
             pltpu.VMEM((ENERGY, 2, 128), f32),
             pltpu.VMEM((1, 128), f32),
             pltpu.VMEM((ENERGY, 1, 128), f32),
+            pltpu.VMEM((POINTS, 128), f32),
             pltpu.VMEM((SLABS, 2, 2, 8, 128), f32),
             pltpu.VMEM((POINTS, 128), f32),
             pltpu.VMEM((2 * POINTS, 128), f32),
@@ -428,6 +437,8 @@
             dma((SLABS, 2)),
             dma((HUBS,)),
             dma((SLABS,)),
+            dma,
+            dma,
             dma,
             dma,
             dma,

time: 36.3 us -> 35.3 us (0.972)
  Pallas kernels: 35.4 us -> 34.4 us
    pallas_call x1, Pallas kernels: 34.8 us -> 33.8 us  [local(): pl.pallas_call(kernel, out_shape=(pltpu.VMEM((2, SLABS, 8, 128), f32), pl...]
where the time goes in v5:
time: 35.3 us; the launch traced here: 35.1 us
  Pallas kernels  34.4 us (97%)
  between operations  0.64 us (2%)
    pallas_call x1, Pallas kernels, local(): pl.pallas_call(kernel, out_shape=(pltpu.VMEM((2, SLABS, 8, 128), f32), pl...  33.8 us

profile of v5, /device:TPU:1, one launch (start us, length us, event | category | flops | bytes accessed | tf_op | source)
XLA Modules:
  0.0 35.1 jit_solution(7514525993872738065)
XLA Ops:
  0.6 33.8 %green_polarization.1 = (f32[2,4,8,128]{3,2,1,0:T(8,128)S(1)}, f32[16,2,128]{2,1,0:T(2,128)S(1)}) custom-call(f32[16,128]{1,0:T(8,128)} %bitcast.15, s32[2]{0:T(128)} %levels_hbm.1, s32[2]{0:T(128)} %jitter_hbm.1, s32[128]{0:T(128)} %offsets_hbm.1, f32[2,2,32,128]{3,2,1,0:T(8,128)} %bitcast.14), custom_call_target="tpu_custom_call" | custom-call | tf_op jit(solution)/shard_map/green_polarization/pallas_call | solution.py:408
  34.5 0.6 %write_out.1 = (f32[2,4,8,128]{3,2,1,0:T(8,128)}, f32[16,2,128]{2,1,0:T(2,128)}) custom-call(f32[2,4,8,128]{3,2,1,0:T(8,128)S(1)} %get-tuple-element.6.dens_ref, f32[16,2,128]{2,1,0:T(2,128)S(1)} %get-tuple-element.7.pol_ref), custom_call_target="tpu_custom_call" | custom-call | tf_op jit(solution)/shard_map/write_out/pallas_call | solution.py:454

commit v6 on v5

--- a/solution.py
+++ b/solution.py
@@ -223,10 +223,9 @@
             for peer in peers:
                 remote(en_row, en_in.at[e], en_send, en_recv, s * ENERGY + peer).start()
 
-        pl.semaphore_wait(barrier, ENERGY - 1)
-
         @pl.when(s == 0)
         def _():
+            pl.semaphore_wait(barrier, ENERGY - 1)
             send_energies()
 
         en_in[e] = en_row[...]
@@ -257,6 +256,12 @@
                     spec[8 * layer + 4 * h + q] = spectral[2 * q : 2 * q + 2, :]
 
 
+            if h == 0:
+
+                @pl.when(s == 1)
+                def _():
+                    pl.semaphore_wait(barrier, ENERGY - 1)
+
             def send_spec(peer):
                 remote(
                     spec.at[lax.rem(peer, BLOCKS)], spec_in.at[e], spec_send, spec_recv, s * ENERGY + peer
@@ -348,7 +353,7 @@
             give(k)
             return carry
 
-        lax.fori_loop(0, BLOCKS - 1, one_offset, 0, unroll=3)
+        lax.fori_loop(0, BLOCKS - 1, one_offset, 0, unroll=9)
         correlate(block)
 
         @pl.when(own == 0)

time: 35.3 us -> 35.2 us (level)
  no operation moved by 1% of the time
where the time goes in v6:
time: 35.2 us; the launch traced here: 34.8 us
  Pallas kernels  34.2 us (97%)
  between operations  0.64 us (2%)
    pallas_call x1, Pallas kernels, local(): pl.pallas_call(kernel, out_shape=(pltpu.VMEM((2, SLABS, 8, 128), f32), pl...  33.5 us

profile of v6, /device:TPU:1, one launch (start us, length us, event | category | flops | bytes accessed | tf_op | source)
XLA Modules:
  0.0 34.8 jit_solution(12778343329348238648)
XLA Ops:
  0.6 33.5 %green_polarization.1 = (f32[2,4,8,128]{3,2,1,0:T(8,128)S(1)}, f32[16,2,128]{2,1,0:T(2,128)S(1)}) custom-call(f32[16,128]{1,0:T(8,128)} %bitcast.15, s32[2]{0:T(128)} %levels_hbm.1, s32[2]{0:T(128)} %jitter_hbm.1, s32[128]{0:T(128)} %offsets_hbm.1, f32[2,2,32,128]{3,2,1,0:T(8,128)} %bitcast.14), custom_call_target="tpu_custom_call" | custom-call | tf_op jit(solution)/shard_map/green_polarization/pallas_call | solution.py:413
  34.2 0.6 %write_out.1 = (f32[2,4,8,128]{3,2,1,0:T(8,128)}, f32[16,2,128]{2,1,0:T(2,128)}) custom-call(f32[2,4,8,128]{3,2,1,0:T(8,128)S(1)} %get-tuple-element.6.dens_ref, f32[16,2,128]{2,1,0:T(2,128)S(1)} %get-tuple-element.7.pol_ref), custom_call_target="tpu_custom_call" | custom-call | tf_op jit(solution)/shard_map/write_out/pallas_call | solution.py:459
